TPU v7x, 512 devices: a whole 4x8x8 slice. The times are simulated.
512 devices in a mesh: sample: 64 (over z, x, core), basis: 8 (over y).
Axes of the slice: x: 4, y: 8, z: 8, core: 2. Of those that a mesh axis runs over, the one named last changes fastest.
Arguments:
- points: float32 [10, 131072], P(None, 'sample'), may hold values from -1 to 1
- run_weights: float32 [131072], P('sample'), may hold values from 0.25 to 6.1
- panel_degrees: int32 [10, 128], P(None, 'basis'), may hold values from 0 to 6, as said below
- trailing_degrees: int32 [10, 2048], P(None, 'basis'), may hold values from 0 to 6, as said below
Outputs:
- r_factor: float32 [128, 128], replicated
- coupling: float32 [128, 2048], P(None, 'basis')
- updated: float32 [131072, 2048], P('sample', 'basis')
Inputs may be any that keep to these rules, and one draw needn't show every extreme that they name: `panel_degrees`: every column is a multi-index of total degree at most 6; all 2176 columns are distinct. `trailing_degrees`: as for panel_degrees; no trailing column repeats a panel column.
All inputs are finite; a program needn't handle non-finite values.
Results may differ from a plain program's by a relative error of at most 0.0003.
Values sent between devices are 32-bit elements; how exact they have to be, the bound alone decides.
A program may use at most 64 MiB of HBM per device.

v0:
```python
import math

import jax
import jax.numpy as jnp
from jax import lax
from jax.sharding import PartitionSpec as P

DEG = 6


def legendre_rows(coord):
    values = [jnp.ones_like(coord), coord]
    for degree in range(1, DEG):
        values.append(
            ((2.0 * degree + 1.0) * coord * values[degree] - degree * values[degree - 1])
            / (degree + 1.0)
        )
    return jnp.stack(
        [values[degree] * math.sqrt(2.0 * degree + 1.0) for degree in range(DEG + 1)], axis=0
    )


def weighted_columns(points, degrees, weights, run_total):
    levels = jnp.arange(DEG + 1, dtype=jnp.int32)
    product = jnp.broadcast_to(
        jnp.sqrt(weights / run_total)[:, None], (weights.shape[0], degrees.shape[1])
    )
    for dim_index in range(points.shape[0]):
        table = legendre_rows(points[dim_index])
        selector = (degrees[dim_index][None, :] == levels[:, None]).astype(jnp.float32)
        product = product * lax.dot_general(
            table, selector, (((0,), (0,)), ((), ())), precision=lax.Precision.HIGHEST
        )
    return product


def inner_products(left, right):
    return lax.dot_general(left, right, (((0,), (0,)), ((), ())), precision=lax.Precision.HIGHEST)


def shards(points, run_weights, panel_degrees, trailing_degrees):
    run_count = points.shape[1] * lax.axis_size("sample")
    run_total = float(run_count)
    own_columns = weighted_columns(points, panel_degrees, run_weights, run_total)
    panel = lax.all_gather(own_columns, "basis", axis=1, tiled=True)
    trailing = weighted_columns(points, trailing_degrees, run_weights, run_total)
    width = panel.shape[1]
    identity = jnp.eye(width, dtype=jnp.float32)
    gram_matrix = lax.psum(inner_products(panel, panel), "sample")
    lower_factor = jnp.linalg.cholesky(gram_matrix)
    inverse_lower = jax.scipy.linalg.solve_triangular(lower_factor, identity, lower=True)
    ortho_rows = lax.dot_general(
        inverse_lower, panel, (((1,), (1,)), ((), ())), precision=lax.Precision.HIGHEST
    )
    local_terms = jnp.dot(ortho_rows, trailing, precision=lax.Precision.HIGHEST)
    coupling = lax.psum(local_terms, "sample")
    updated = (trailing - inner_products(ortho_rows, coupling)) * math.sqrt(run_count)
    return (lower_factor.T, coupling, updated)


def solution(mesh):
    in_specs = (P(None, "sample"), P("sample"), P(None, "basis"), P(None, "basis"))
    out_specs = (P(), P(None, "basis"), P("sample", "basis"))
    return jax.shard_map(shards, mesh=mesh, in_specs=in_specs, out_specs=out_specs, check_vma=False)
```

profile of v0, /device:TPU:1, one launch (start us, length us, event | category | flops | bytes accessed | tf_op | source)
XLA Modules:
  0.0 468.8 jit_solution(5039410544258902816)
XLA Ops:
  7.2 1.5 broadcast_multiply_fusion.40
  8.7 2.1 subtract_multiply_fusion
  10.8 1.0 slice_bitcast_fusion
  11.8 0.7 multiply_sqrt_fusion
  16.3 0.9 convolution_multiply_fusion.10
  17.5 1.2 convolution_multiply_fusion.9
  18.7 1.0 convolution_multiply_fusion.8
  19.7 1.0 convolution_multiply_fusion.7
  20.8 1.0 convolution_multiply_fusion.6
  21.8 1.0 convolution_multiply_fusion.5
  22.9 1.0 convolution_multiply_fusion.4
  23.9 1.0 convolution_multiply_fusion.3
  25.0 1.0 convolution_multiply_fusion.2
  26.0 2.4 convolution_multiply_fusion.1
  28.4 30.6 %all-gather.2.cloned.1.call-done = f32[2048,128]{0,1:T(8,128)} async-done(((f32[2048,16]{0,1:T(8,128)}), f32[2048,128]{0,1:T(8,128)}) %all-gather.2.cloned.1.call-update) | async-done | bytes 1048592 | tf_op jit(solution)/shard_map/all_gather | solution.py:45
  59.0 3.2 fusion.36
  62.2 0.3 all-reduce.5.cloned.1.call-start
  62.5 2.7 convolution_multiply_fusion
  65.2 181.5 %all-reduce.3.cloned.1.call-done = f32[128,128]{0,1:T(8,128)} async-done(((f32[128,128]{0,1:T(8,128)}), f32[128,128]{0,1:T(8,128)}) %all-reduce.3.cloned.1.call-update) | async-done | bytes 65552 | tf_op jit(solution)/shard_map/psum | solution.py:49
  246.7 0.9 copy.8
  247.6 0.9 fusion.3
  248.5 11.7 %cholesky.20 = f32[128,128]{1,0:T(8,128)S(1)} custom-call(f32[128,128]{1,0:T(8,128)S(1)} %fusion.3), custom_call_target="Cholesky" | custom-call | tf_op jit(solution)/shard_map/jit(cholesky)/cholesky | solution.py:50
  260.2 0.6 compare_reduce_fusion
  260.9 0.7 select_bitcast_fusion
  261.6 9.8 %custom-call.7 = f32[1,128,128]{1,2,0:T(8,128)S(1)} custom-call(f32[1,128,128]{2,1,0:T(8,128)S(1)} %get-tuple-element.102), custom_call_target="InvertDiagBlocksLowerTriangular" | custom-call | tf_op jit(solution)/shard_map/jit(_solve_triangular)/triangular_solve | solution.py:51
  271.6 1.0 fusion.37
  272.7 1.0 copy-done.1
  273.6 1.8 fusion.38
  275.5 0.7 copy.9
  276.2 181.0 %all-reduce.5.cloned.1.call-done = f32[128,256]{1,0:T(8,128)} async-done(((f32[128,256]{1,0:T(8,128)}), f32[128,256]{1,0:T(8,128)}) %all-reduce.5.cloned.1.call-update) | async-done | bytes 131088 | tf_op jit(solution)/shard_map/psum | solution.py:56
  457.2 4.4 fusion
  461.6 0.7 copy.13
  (50 shorter events, 4.2 us)
Async XLA Ops:
  7.2 51.9 %all-gather.2.cloned.1.call-start = ((), (), s32[]{:S(2)}) async-start(), calls=%async_computation | async-start | bytes 1179648 | tf_op jit(solution)/shard_map/all_gather | solution.py:45
  13.4 4.1 copy-start.3
  17.2 229.5 %all-reduce.3.cloned.1.call-start = ((), (), s32[]{:S(2)}) async-start(), calls=%async_computation.1 | async-start | bytes 131072 | tf_op jit(solution)/shard_map/psum | solution.py:49
  62.2 394.9 %all-reduce.5.cloned.1.call-start = ((), (), s32[]{:S(2)}) async-start(), calls=%async_computation.2 | async-start | bytes 262144 | tf_op jit(solution)/shard_map/psum | solution.py:56
  62.5 209.1 %copy-start = (f32[2048,128]{0,1:T(8,128)S(1)}, f32[2048,128]{0,1:T(8,128)}, u32[]{:S(2)}) copy-start(f32[2048,128]{0,1:T(8,128)} %all-gather.2.cloned.1.call-done) | copy-start | bytes 3145732
  272.6 1.0 copy-start.1
  457.1 4.4 copy-start.2
Sparse Core Ops, SparseCore 0:
  17.3 41.6 all-gather.1
  63.1 183.6 all-reduce.2
  275.6 181.5 all-reduce.4
where the time goes:
time: 469 us
  waiting for transfers between devices  393 us (84%)
  other arithmetic  28.3 us (6%)
  matrix products  27.5 us (6%)
  between operations  14.1 us (3%)
  local copies, waits for them, and re-layouts  5.28 us (1%)
    psum x1, waiting for transfers between devices, shards(): gram_matrix = lax.psum(inner_products(panel, panel), 'sample')  181 us
    psum x1, waiting for transfers between devices, shards(): coupling = lax.psum(local_terms, 'sample')  181 us
    all_gather x1, waiting for transfers between devices, shards(): panel = lax.all_gather(own_columns, 'basis', axis=1, tiled=True)  30.6 us
    dot_general x20, matrix products, weighted_columns(): lax.dot_general(table, selector, (((0,), (0,)), ((), ())), precision=lax....  16.8 us
    another operation x3, other arithmetic, shards(): lower_factor = jnp.linalg.cholesky(gram_matrix)  12.4 us
    another operation x2, other arithmetic, shards(): jax.scipy.linalg.solve_triangular(lower_factor, identity, lower=True)  10.5 us
  transfers between devices with their start and end apart: 3, of which 3 were waited for; matrix products, arithmetic and copies ran while one was open for 3% of the time, Pallas kernels for 0%

commit v1 on v0

v1 whole, which is shorter than its diff:
```python
import functools
import math

import jax
import jax.numpy as jnp
from jax import lax
from jax.experimental import pallas as pl
from jax.experimental.pallas import tpu as pltpu
from jax.sharding import PartitionSpec as P

DEG = 6
LEVELS = DEG + 1
TILES = 16
PANEL = 128
TRAIL = 256
COLS = PANEL + TRAIL
RING = 8
MESH = pl.DeviceIdType.MESH
HIGHEST = lax.Precision.HIGHEST
NT = (((1,), (1,)), ((), ()))
TN = (((0,), (0,)), ((), ()))


def dot(left, right, dims):
    return lax.dot_general(left, right, dims, precision=HIGHEST, preferred_element_type=jnp.float32)


def lane_splat(row, lane):
    return jnp.broadcast_to(row[:, lane:lane + 1], (8, 128))


def sublane_splat(row, sublane):
    return jnp.broadcast_to(row[sublane:sublane + 1, :], (8, 128))


def cholesky(gram_ref, upper_ref, inverse_ref):
    sub = lax.broadcasted_iota(jnp.int32, (8, 128), 0)
    lane = lax.broadcasted_iota(jnp.int32, (8, 128), 1)
    gram = [gram_ref[8 * i:8 * i + 8, :] for i in range(16)]
    ident = [jnp.where(lane == sub + 8 * i, 1.0, 0.0) for i in range(16)]
    for k in range(16):
        splats = [lane_splat(gram[k], 8 * k + j) for j in range(8)]
        diag = [[sublane_splat(splats[j], i) if i >= j else None for j in range(8)] for i in range(8)]
        low = [[None] * 8 for _ in range(8)]
        inv = [None] * 8
        for j in range(8):
            inv[j] = lax.rsqrt(diag[j][j])
            for i in range(j + 1, 8):
                low[i][j] = diag[i][j] * inv[j]
            for i in range(j + 1, 8):
                for m in range(i, 8):
                    diag[m][i] = diag[m][i] - low[m][j] * low[i][j]
        up, lo = [], []
        for j in range(8):
            a, b = sublane_splat(gram[k], j), sublane_splat(ident[k], j)
            for i in range(j):
                a = a - low[j][i] * up[i]
                b = b - low[j][i] * lo[i]
            up.append(a * inv[j])
            lo.append(b * inv[j])
        up_rows, lo_rows = up[0], lo[0]
        for j in range(1, 8):
            up_rows = jnp.where(sub == j, up[j], up_rows)
            lo_rows = jnp.where(sub == j, lo[j], lo_rows)
        upper_ref[8 * k:8 * k + 8, :] = jnp.where(lane >= sub + 8 * k, up_rows, 0.0)
        inverse_ref[8 * k:8 * k + 8, :] = lo_rows
        if k == 15:
            break
        for j in reversed(range(8)):
            for i in range(j + 1, 8):
                up[j] = up[j] - low[i][j] * up[i]
                lo[j] = lo[j] - low[i][j] * lo[i]
            up[j] = up[j] * inv[j]
            lo[j] = lo[j] * inv[j]
        for i in range(k + 1, 16):
            for j in range(8):
                c = lane_splat(gram[i], 8 * k + j)
                if j == 0:
                    a, b = c * up[0], c * lo[0]
                else:
                    a, b = a + c * up[j], b + c * lo[j]
            gram[i] = gram[i] - a
            ident[i] = ident[i] - b


def legendre(coord):
    values = [jnp.ones_like(coord), coord]
    for k in range(1, DEG):
        values.append(((2.0 * k + 1.0) * coord * values[k] - k * values[k - 1]) * (1.0 / (k + 1.0)))
    return [values[k] * math.sqrt(2.0 * k + 1.0) for k in range(LEVELS)]


def fill_tables(coords_ref, weight, triples, pairs):
    for group, table in enumerate(triples):
        first, second, third = (legendre(coords_ref[3 * group + d]) for d in range(3))
        for a in range(LEVELS):
            for b in range(LEVELS - a):
                head = first[a] * second[b]
                for c in range(LEVELS - a - b):
                    table[a * 49 + b * 7 + c] = head * third[c]
    for group, table in enumerate(pairs):
        first, second = (legendre(coords_ref[6 + 2 * group + d]) for d in range(2))
        if group == 0:
            first = [value * weight for value in first]
        for a in range(LEVELS):
            for b in range(LEVELS - a):
                table[a * 7 + b] = first[a] * second[b]


def table_rows(degree):
    return [
        degree(0) * 49 + degree(1) * 7 + degree(2),
        degree(3) * 49 + degree(4) * 7 + degree(5),
        degree(6) * 7 + degree(7),
        degree(8) * 7 + degree(9),
    ]


def kernel(run_total, points_ref, weights_ref, panel_deg_ref, trail_deg_ref,
           upper_out, coupling_out, updated_out,
           coords, triple_a, triple_b, pair_a, pair_b, columns,
           trail_idx_v, trail_idx, panel_degs, panel_idx_v, panel_idx,
           trail_t, panel_t, out_buf,
           gram_x, gram_land, gram_z, gram_all, cross_x, cross_land, cross_z, cross_all,
           inverse, local_sem, deg_send, deg_recv, send_sem, recv_sem, out_sem):
    s, y = lax.axis_index("sample"), lax.axis_index("basis")
    z, q = s // RING, lax.rem(s, RING)
    others = range(1, RING)
    y_peers = [(s, lax.rem(y + k, RING)) for k in others]
    q_peers = [(z * RING + lax.rem(q + k, RING), y) for k in others]
    z_peers = [(lax.rem(z + k, RING) * RING + q, y) for k in others]

    barrier = pltpu.get_barrier_semaphore()
    for peer in y_peers + z_peers + q_peers:
        pl.semaphore_signal(barrier, inc=1, device_id=peer, device_id_type=MESH)

    def send(src, dst, ssem, rsem, peer):
        pltpu.make_async_remote_copy(
            src_ref=src, dst_ref=dst, send_sem=ssem, recv_sem=rsem, device_id=peer, device_id_type=MESH
        ).start()

    def wait(ref, sem):
        pltpu.make_async_copy(ref, ref, sem).wait()

    for g, row in enumerate(table_rows(lambda d: trail_deg_ref[d:d + 1, :])):
        trail_idx_v[g:g + 1, :] = row
    idx_copy = pltpu.make_async_copy(trail_idx_v, trail_idx, local_sem)
    idx_copy.start()
    for r in range(TILES):
        coords[:, r, :] = points_ref[:, 128 * r:128 * r + 128]
    weight = jnp.sqrt(weights_ref[...] / run_total)
    fill_tables(coords, weight, (triple_a, triple_b), (pair_a, pair_b))
    idx_copy.wait()

    pl.semaphore_wait(barrier, 3 * (RING - 1))
    for peer in y_peers:
        send(panel_deg_ref, panel_degs.at[y], deg_send, deg_recv, peer)
    panel_degs[y] = panel_deg_ref[...]

    def product(i, j, k, m):
        return triple_a[i] * triple_b[j] * (pair_a[k] * pair_b[m])

    def trail_column(j, carry):
        value = product(trail_idx[0, j], trail_idx[1, j], trail_idx[2, j], trail_idx[3, j])
        columns[pl.ds(PANEL + j, TILES, stride=COLS), :] = value
        return carry

    lax.fori_loop(0, TRAIL, trail_column, 0, unroll=8)

    wait(panel_degs.at[pl.ds(0, RING - 1)], deg_recv)
    for g, rows in enumerate(table_rows(lambda d: panel_degs[:, d, :])):
        panel_idx_v[g] = rows
    panel_copy = pltpu.make_async_copy(panel_idx_v, panel_idx, local_sem)
    panel_copy.start()
    panel_copy.wait()

    def panel_column(o, carry):
        for i in range(16):
            value = product(panel_idx[0, o, i], panel_idx[1, o, i], panel_idx[2, o, i], panel_idx[3, o, i])
            columns[pl.ds(o * 16 + i, TILES, stride=COLS), :] = value
        return carry

    lax.fori_loop(0, RING, panel_column, 0)

    def block(start, size, r):
        return jnp.concatenate(
            [columns[pl.ds((2 * r + h) * COLS + start, size), :] for h in range(2)], axis=1
        )

    def phase_one(x, land, i):
        for k in others:
            send(x.at[lax.rem(q + k, RING)], land.at[k - 1], send_sem.at[i], recv_sem.at[i], q_peers[k - 1])

    def phase_two(x, land, all_z, i):
        wait(land, recv_sem.at[i])
        part = x[q]
        for k in range(RING - 1):
            part = part + land[k]
        all_z[z] = part
        for peer in z_peers:
            send(all_z.at[z], all_z.at[z], send_sem.at[i + 1], recv_sem.at[i + 1], peer)

    def phase_three(land, all_z, out, i):
        wait(land, recv_sem.at[i + 1])
        total = all_z[0]
        for k in others:
            total = total + all_z[k]
        out[q] = total
        for peer in q_peers:
            send(out.at[q], out.at[q], send_sem.at[i + 2], recv_sem.at[i + 2], peer)

    gram = jnp.zeros((PANEL, PANEL), jnp.float32)
    for r in range(TILES // 2):
        panel = block(0, PANEL, r)
        gram = gram + dot(panel, panel, NT)
    gram_x[...] = gram.reshape(gram_x.shape)
    phase_one(gram_x, gram_land, 0)
    cross = jnp.zeros((PANEL, TRAIL), jnp.float32)
    for r in range(TILES // 2):
        cross = cross + dot(block(0, PANEL, r), block(PANEL, TRAIL, r), NT)
    cross_x[...] = cross.reshape(cross_x.shape)
    phase_one(cross_x, cross_land, 3)

    def transpose(r, carry):
        rows = pl.ds(pl.multiple_of(r * 128, 128), 128)
        base = pl.multiple_of(r * COLS, 128)
        panel_t[rows, :] = columns[pl.ds(base, PANEL), :].T
        trail_t[rows, :] = columns[pl.ds(base + PANEL, TRAIL), :].T
        return carry

    lax.fori_loop(0, TILES, transpose, 0)
    phase_two(gram_x, gram_land, gram_z, 0)
    phase_two(cross_x, cross_land, cross_z, 3)
    phase_three(gram_land, gram_z, gram_all, 0)
    phase_three(cross_land, cross_z, cross_all, 3)

    wait(gram_land, recv_sem.at[2])
    gram_flat = gram_all.reshape(PANEL, PANEL)
    cholesky(gram_flat, upper_out, inverse)
    wait(cross_land, recv_sem.at[5])
    coupling = dot(inverse[...], cross_all[...].reshape(PANEL, TRAIL), (((1,), (0,)), ((), ())))
    coupling_out[...] = coupling
    weights = dot(inverse[...], coupling, TN)
    scale = math.sqrt(run_total)
    part = 2048 // 4
    for p in range(4):
        rows = pl.ds(p * part, part)
        out_buf[rows, :] = (trail_t[rows, :] - dot(panel_t[rows, :], weights, (((1,), (0,)), ((), ())))) * scale
        pltpu.make_async_copy(out_buf.at[rows, :], updated_out.at[rows, :], out_sem).start()
    wait(panel_degs.at[pl.ds(0, RING - 1)], deg_send)
    for i in range(3):
        wait(gram_land, send_sem.at[i])
        wait(cross_land, send_sem.at[i + 3])
    pltpu.make_async_copy(out_buf, updated_out, out_sem).wait()


def shards(points, run_weights, panel_degrees, trailing_degrees):
    run_total = float(points.shape[1] * lax.axis_size("sample"))
    f32, i32 = jnp.float32, jnp.int32
    vmem = pl.BlockSpec(memory_space=pltpu.VMEM)
    dma = pltpu.SemaphoreType.DMA
    chunk, wide = (16, PANEL), (16, TRAIL)
    return pl.pallas_call(
        functools.partial(kernel, run_total),
        out_shape=[
            jax.ShapeDtypeStruct((PANEL, PANEL), f32),
            jax.ShapeDtypeStruct((PANEL, TRAIL), f32),
            jax.ShapeDtypeStruct((2048, TRAIL), f32),
        ],
        in_specs=[vmem] * 4,
        out_specs=[vmem, vmem, pl.BlockSpec(memory_space=pl.ANY)],
        scratch_shapes=[
            pltpu.VMEM((10, TILES, 128), f32),
            pltpu.VMEM((343, TILES, 128), f32),
            pltpu.VMEM((343, TILES, 128), f32),
            pltpu.VMEM((49, TILES, 128), f32),
            pltpu.VMEM((49, TILES, 128), f32),
            pltpu.VMEM((TILES * COLS, 128), f32),
            pltpu.VMEM((4, TRAIL), i32),
            pltpu.SMEM((4, TRAIL), i32),
            pltpu.VMEM((RING, 10, 16), i32),
            pltpu.VMEM((4, RING, 16), i32),
            pltpu.SMEM((4, RING, 16), i32),
            pltpu.VMEM((2048, TRAIL), f32),
            pltpu.VMEM((2048, PANEL), f32),
            pltpu.VMEM((2048, TRAIL), f32),
            pltpu.VMEM((RING,) + chunk, f32),
            pltpu.VMEM((RING - 1,) + chunk, f32),
            pltpu.VMEM((RING,) + chunk, f32),
            pltpu.VMEM((RING,) + chunk, f32),
            pltpu.VMEM((RING,) + wide, f32),
            pltpu.VMEM((RING - 1,) + wide, f32),
            pltpu.VMEM((RING,) + wide, f32),
            pltpu.VMEM((RING,) + wide, f32),
            pltpu.VMEM((PANEL, PANEL), f32),
            dma,
            dma,
            dma,
            dma((6,)),
            dma((6,)),
            dma,
        ],
        name="panel_step",
        compiler_params=pltpu.CompilerParams(
            collective_id=0, has_side_effects=True, vmem_limit_bytes=40 * 2**20
        ),
    )(points, run_weights.reshape(TILES, 128), panel_degrees, trailing_degrees)


def solution(mesh):
    in_specs = (P(None, "sample"), P("sample"), P(None, "basis"), P(None, "basis"))
    out_specs = (P(), P(None, "basis"), P("sample", "basis"))
    return jax.shard_map(shards, mesh=mesh, in_specs=in_specs, out_specs=out_specs, check_vma=False)
```

time: 469 us -> 54.9 us (0.12)
  waiting for transfers between devices: 393 us -> 0 us
  Pallas kernels: 0 us -> 48.3 us
  other arithmetic: 28.3 us -> 0 us
  matrix products: 27.5 us -> 0 us
  between operations: 14.1 us -> 0.65 us
    psum x2 -> x0, waiting for transfers between devices: 362 us -> none  [the longest x1 181 us: shards(): gram_matrix = lax.psum(inner_products(panel, panel), 'sample')]
    pallas_call x0 -> x1, Pallas kernels: none -> 48.3 us  [shards(): pl.pallas_call(functools.partial(kernel, run_total), out_shape=[jax.Shape...]
    all_gather x1 -> x0, waiting for transfers between devices: 30.6 us -> none  [shards(): panel = lax.all_gather(own_columns, 'basis', axis=1, tiled=True)]
    dot_general x24 -> x0, matrix products: 27.2 us -> none  [the longest x20 16.8 us: weighted_columns(): lax.dot_general(table, selector, (((0,), (0,)), ((), ())), precision=lax....]
    another operation x5 -> x0, other arithmetic: 22.9 us -> none  [the longest x3 12.4 us: shards(): lower_factor = jnp.linalg.cholesky(gram_matrix)]
  transfers between devices with their start and end apart: 3 -> 0, of which waited for: 3 -> 0; matrix products, arithmetic and copies ran while one was open for 3% -> 0% of each run, Pallas kernels for 0% -> 0%
where the time goes in v1:
time: 54.9 us; the launch traced here: 54.6 us
  Pallas kernels  48.3 us (88%)
  local copies, waits for them, and re-layouts  5.61 us (10%)
  between operations  0.65 us (1%)
    pallas_call x1, Pallas kernels, shards(): pl.pallas_call(functools.partial(kernel, run_total), out_shape=[jax.Shape...  48.3 us
    unnamed x11, local copies, waits for them, and re-layouts  5.61 us

profile of v1, /device:TPU:1, one launch (start us, length us, event | category | flops | bytes accessed | tf_op | source)
XLA Modules:
  0.0 54.6 jit_solution(17245220259186327996)
XLA Ops:
  0.6 0.0 copy-start
  0.6 0.9 %copy-done = f32[10,2048]{1,0:T(8,128)S(1)} copy-done((f32[10,2048]{1,0:T(8,128)S(1)}, f32[10,2048]{1,0:T(8,128)}, u32[]{:S(2)}) %copy-start) | copy-done | bytes 81944
  1.5 0.0 copy-start.1
  1.5 0.7 %copy-done.1 = s32[10,256]{1,0:T(8,128)S(1)} copy-done((s32[10,256]{1,0:T(8,128)S(1)}, s32[10,256]{1,0:T(8,128)}, u32[]{:S(2)}) %copy-start.1) | copy-done | bytes 10264
  2.3 0.0 copy-start.2
  2.3 0.7 %copy-done.2 = f32[2048]{0:T(1024)S(1)} copy-done((f32[2048]{0:T(1024)S(1)}, f32[2048]{0:T(1024)}, u32[]{:S(2)}) %copy-start.2) | copy-done | bytes 8216
  3.0 0.0 copy-start.3
  3.0 0.7 %copy-done.3 = s32[10,16]{1,0:T(8,128)S(1)} copy-done((s32[10,16]{1,0:T(8,128)S(1)}, s32[10,16]{1,0:T(8,128)}, u32[]{:S(2)}) %copy-start.3) | copy-done | bytes 664
  3.6 48.3 %panel_step.1 = (f32[128,128]{1,0:T(8,128)S(1)}, f32[128,256]{1,0:T(8,128)S(1)}, f32[2048,256]{1,0:T(8,128)S(1)}) custom-call(f32[10,2048]{1,0:T(8,128)S(1)} %copy-done, f32[16,128]{1,0:T(8,128)S(1)} %bitcast.1, s32[10,16]{1,0:T(8,128)S(1)} %copy-done.3, s32[10,256]{1,0:T(8,128)S(1)} %copy-done.1), custom_call_target="tpu_custom_call" | custom-call | tf_op jit(solution)/shard_map/panel_step/pallas_call | solution.py:263
  52.0 0.6 %copy.10 = f32[128,128]{1,0:T(8,128)} copy(f32[128,128]{1,0:T(8,128)S(1)} %get-tuple-element.6) | data formatting | bytes 131072
  52.6 0.7 %copy.11 = f32[128,256]{1,0:T(8,128)} copy(f32[128,256]{1,0:T(8,128)S(1)} %get-tuple-element.7) | data formatting | bytes 262144
  53.2 1.3 %copy.12 = f32[2048,256]{1,0:T(8,128)} copy(f32[2048,256]{1,0:T(8,128)S(1)} %get-tuple-element.8) | data formatting | bytes 4194304
Async XLA Ops:
  0.6 0.9 %copy-start = (f32[10,2048]{1,0:T(8,128)S(1)}, f32[10,2048]{1,0:T(8,128)}, u32[]{:S(2)}) copy-start(f32[10,2048]{1,0:T(8,128)} %points_ref.1) | copy-start | bytes 245764
  1.5 0.7 %copy-start.1 = (s32[10,256]{1,0:T(8,128)S(1)}, s32[10,256]{1,0:T(8,128)}, u32[]{:S(2)}) copy-start(s32[10,256]{1,0:T(8,128)} %trail_deg_ref.1) | copy-start | bytes 30724
  2.3 0.7 %copy-start.2 = (f32[2048]{0:T(1024)S(1)}, f32[2048]{0:T(1024)}, u32[]{:S(2)}) copy-start(f32[2048]{0:T(1024)} %param.5) | copy-start | bytes 24580
  3.0 0.7 %copy-start.3 = (s32[10,16]{1,0:T(8,128)S(1)}, s32[10,16]{1,0:T(8,128)}, u32[]{:S(2)}) copy-start(s32[10,16]{1,0:T(8,128)} %panel_deg_ref.1) | copy-start | bytes 1924

commit v2 on v1

--- a/solution.py
+++ b/solution.py
@@ -17,6 +17,7 @@
 RING = 8
 MESH = pl.DeviceIdType.MESH
 HIGHEST = lax.Precision.HIGHEST
+NN = (((1,), (0,)), ((), ()))
 NT = (((1,), (1,)), ((), ()))
 TN = (((0,), (0,)), ((), ()))
 
@@ -116,13 +117,22 @@
     ]
 
 
+def split(value):
+    high = value.astype(jnp.bfloat16)
+    return high, (value - high.astype(jnp.float32)).astype(jnp.bfloat16)
+
+
+def fast_dot(left, right, dims):
+    return lax.dot_general(left, right, dims, preferred_element_type=jnp.float32)
+
+
 def kernel(run_total, points_ref, weights_ref, panel_deg_ref, trail_deg_ref,
-           upper_out, coupling_out, updated_out,
+           upper_out, coupling_out, weights_out, trail_t, panel_t,
+           points_v, weights_v, panel_deg_v, trail_deg_v,
            coords, triple_a, triple_b, pair_a, pair_b, columns,
            trail_idx_v, trail_idx, panel_degs, panel_idx_v, panel_idx,
-           trail_t, panel_t, out_buf,
            gram_x, gram_land, gram_z, gram_all, cross_x, cross_land, cross_z, cross_all,
-           inverse, local_sem, deg_send, deg_recv, send_sem, recv_sem, out_sem):
+           inverse, in_sem, local_sem, deg_send, deg_recv, send_sem, recv_sem):
     s, y = lax.axis_index("sample"), lax.axis_index("basis")
     z, q = s // RING, lax.rem(s, RING)
     others = range(1, RING)
@@ -133,6 +143,14 @@
     barrier = pltpu.get_barrier_semaphore()
     for peer in y_peers + z_peers + q_peers:
         pl.semaphore_signal(barrier, inc=1, device_id=peer, device_id_type=MESH)
+    loads = [
+        pltpu.make_async_copy(src, dst, in_sem.at[i])
+        for i, (src, dst) in enumerate([
+            (panel_deg_ref, panel_deg_v), (trail_deg_ref, trail_deg_v), (points_ref, points_v), (weights_ref, weights_v)
+        ])
+    ]
+    for load in loads:
+        load.start()
 
     def send(src, dst, ssem, rsem, peer):
         pltpu.make_async_remote_copy(
@@ -142,20 +160,24 @@
     def wait(ref, sem):
         pltpu.make_async_copy(ref, ref, sem).wait()
 
-    for g, row in enumerate(table_rows(lambda d: trail_deg_ref[d:d + 1, :])):
+    loads[0].wait()
+    pl.semaphore_wait(barrier, 3 * (RING - 1))
+    for peer in y_peers:
+        send(panel_deg_v, panel_degs.at[y], deg_send, deg_recv, peer)
+    panel_degs[y] = panel_deg_v[...]
+
+    loads[1].wait()
+    for g, row in enumerate(table_rows(lambda d: trail_deg_v[d:d + 1, :])):
         trail_idx_v[g:g + 1, :] = row
     idx_copy = pltpu.make_async_copy(trail_idx_v, trail_idx, local_sem)
     idx_copy.start()
+    loads[2].wait()
+    loads[3].wait()
     for r in range(TILES):
-        coords[:, r, :] = points_ref[:, 128 * r:128 * r + 128]
-    weight = jnp.sqrt(weights_ref[...] / run_total)
+        coords[:, r, :] = points_v[:, 128 * r:128 * r + 128]
+    weight = jnp.sqrt(weights_v[...] / run_total)
     fill_tables(coords, weight, (triple_a, triple_b), (pair_a, pair_b))
     idx_copy.wait()
-
-    pl.semaphore_wait(barrier, 3 * (RING - 1))
-    for peer in y_peers:
-        send(panel_deg_ref, panel_degs.at[y], deg_send, deg_recv, peer)
-    panel_degs[y] = panel_deg_ref[...]
 
     def product(i, j, k, m):
         return triple_a[i] * triple_b[j] * (pair_a[k] * pair_b[m])
@@ -166,6 +188,15 @@
         return carry
 
     lax.fori_loop(0, TRAIL, trail_column, 0, unroll=8)
+    scale = math.sqrt(run_total)
+
+    def transpose_trail(r, carry):
+        rows = pl.ds(pl.multiple_of(r * 128, 128), 128)
+        base = pl.multiple_of(r * COLS, 128)
+        trail_t[rows, :] = columns[pl.ds(base + PANEL, TRAIL), :].T * scale
+        return carry
+
+    lax.fori_loop(0, TILES, transpose_trail, 0)
 
     wait(panel_degs.at[pl.ds(0, RING - 1)], deg_recv)
     for g, rows in enumerate(table_rows(lambda d: panel_degs[:, d, :])):
@@ -183,9 +214,14 @@
     lax.fori_loop(0, RING, panel_column, 0)
 
     def block(start, size, r):
-        return jnp.concatenate(
+        high, low = split(jnp.concatenate(
             [columns[pl.ds((2 * r + h) * COLS + start, size), :] for h in range(2)], axis=1
-        )
+        ))
+        return jnp.concatenate([high, low], axis=0)
+
+    def quadrants(total):
+        rows, cols = total.shape[0] // 2, total.shape[1] // 2
+        return (total[rows:, cols:] + (total[:rows, cols:] + total[rows:, :cols])) + total[:rows, :cols]
 
     def phase_one(x, land, i):
         for k in others:
@@ -209,67 +245,83 @@
         for peer in q_peers:
             send(out.at[q], out.at[q], send_sem.at[i + 2], recv_sem.at[i + 2], peer)
 
-    gram = jnp.zeros((PANEL, PANEL), jnp.float32)
+    panels = [block(0, PANEL, r) for r in range(TILES // 2)]
+    gram = fast_dot(panels[0], panels[0], NT)
+    for r in range(1, TILES // 2):
+        gram = gram + fast_dot(panels[r], panels[r], NT)
+    gram_x[...] = quadrants(gram).reshape(gram_x.shape)
+    phase_one(gram_x, gram_land, 0)
+    cross = jnp.zeros((2 * PANEL, 2 * TRAIL), jnp.float32)
     for r in range(TILES // 2):
-        panel = block(0, PANEL, r)
-        gram = gram + dot(panel, panel, NT)
-    gram_x[...] = gram.reshape(gram_x.shape)
-    phase_one(gram_x, gram_land, 0)
-    cross = jnp.zeros((PANEL, TRAIL), jnp.float32)
-    for r in range(TILES // 2):
-        cross = cross + dot(block(0, PANEL, r), block(PANEL, TRAIL, r), NT)
-    cross_x[...] = cross.reshape(cross_x.shape)
+        cross = cross + fast_dot(panels[r], block(PANEL, TRAIL, r), NT)
+    cross_x[...] = quadrants(cross).reshape(cross_x.shape)
     phase_one(cross_x, cross_land, 3)
 
-    def transpose(r, carry):
+    def transpose_panel(r, carry):
         rows = pl.ds(pl.multiple_of(r * 128, 128), 128)
         base = pl.multiple_of(r * COLS, 128)
-        panel_t[rows, :] = columns[pl.ds(base, PANEL), :].T
-        trail_t[rows, :] = columns[pl.ds(base + PANEL, TRAIL), :].T
+        high, low = split(columns[pl.ds(base, PANEL), :].T)
+        panel_t[rows, :] = jnp.concatenate([high, low], axis=1)
         return carry
 
-    lax.fori_loop(0, TILES, transpose, 0)
+    lax.fori_loop(0, TILES, transpose_panel, 0)
     phase_two(gram_x, gram_land, gram_z, 0)
     phase_two(cross_x, cross_land, cross_z, 3)
     phase_three(gram_land, gram_z, gram_all, 0)
     phase_three(cross_land, cross_z, cross_all, 3)
 
     wait(gram_land, recv_sem.at[2])
-    gram_flat = gram_all.reshape(PANEL, PANEL)
-    cholesky(gram_flat, upper_out, inverse)
+    cholesky(gram_all.reshape(PANEL, PANEL), upper_out, inverse)
     wait(cross_land, recv_sem.at[5])
-    coupling = dot(inverse[...], cross_all[...].reshape(PANEL, TRAIL), (((1,), (0,)), ((), ())))
+    coupling = dot(inverse[...], cross_all[...].reshape(PANEL, TRAIL), NN)
     coupling_out[...] = coupling
-    weights = dot(inverse[...], coupling, TN)
-    scale = math.sqrt(run_total)
-    part = 2048 // 4
-    for p in range(4):
-        rows = pl.ds(p * part, part)
-        out_buf[rows, :] = (trail_t[rows, :] - dot(panel_t[rows, :], weights, (((1,), (0,)), ((), ())))) * scale
-        pltpu.make_async_copy(out_buf.at[rows, :], updated_out.at[rows, :], out_sem).start()
+    weights_out[...] = dot(inverse[...], coupling, TN) * -scale
     wait(panel_degs.at[pl.ds(0, RING - 1)], deg_send)
     for i in range(3):
         wait(gram_land, send_sem.at[i])
         wait(cross_land, send_sem.at[i + 3])
-    pltpu.make_async_copy(out_buf, updated_out, out_sem).wait()
+
+
+def update_kernel(upper_ref, coupling_ref, weights_ref, trail_t, panel_t, upper_out, coupling_out, updated_out, buf, sem):
+    small = [
+        pltpu.make_async_copy(upper_ref, upper_out, sem.at[0]),
+        pltpu.make_async_copy(coupling_ref, coupling_out, sem.at[1]),
+    ]
+    for copy in small:
+        copy.start()
+    high, low = split(weights_ref[...])
+    both = jnp.concatenate([high, high], axis=0)
+    part = 2048 // 4
+    large = []
+    for p in range(4):
+        rows = pl.ds(p * part, part)
+        panel = panel_t[rows, :]
+        buf[rows, :] = trail_t[rows, :] + (fast_dot(panel[:, :PANEL], low, NN) + fast_dot(panel, both, NN))
+        large.append(pltpu.make_async_copy(buf.at[rows, :], updated_out.at[rows, :], sem.at[2 + p]))
+        large[-1].start()
+    for copy in small + large:
+        copy.wait()
 
 
 def shards(points, run_weights, panel_degrees, trailing_degrees):
     run_total = float(points.shape[1] * lax.axis_size("sample"))
     f32, i32 = jnp.float32, jnp.int32
-    vmem = pl.BlockSpec(memory_space=pltpu.VMEM)
+    vmem, hbm = pl.BlockSpec(memory_space=pltpu.VMEM), pl.BlockSpec(memory_space=pltpu.HBM)
     dma = pltpu.SemaphoreType.DMA
     chunk, wide = (16, PANEL), (16, TRAIL)
-    return pl.pallas_call(
+    upper = jax.ShapeDtypeStruct((PANEL, PANEL), f32)
+    coupling = jax.ShapeDtypeStruct((PANEL, TRAIL), f32)
+    updated = jax.ShapeDtypeStruct((2048, TRAIL), f32)
+    parts = pl.pallas_call(
         functools.partial(kernel, run_total),
-        out_shape=[
-            jax.ShapeDtypeStruct((PANEL, PANEL), f32),
-            jax.ShapeDtypeStruct((PANEL, TRAIL), f32),
-            jax.ShapeDtypeStruct((2048, TRAIL), f32),
-        ],
-        in_specs=[vmem] * 4,
-        out_specs=[vmem, vmem, pl.BlockSpec(memory_space=pl.ANY)],
+        out_shape=[upper, coupling, coupling, updated, jax.ShapeDtypeStruct((2048, 2 * PANEL), jnp.bfloat16)],
+        in_specs=[hbm] * 4,
+        out_specs=[vmem] * 5,
         scratch_shapes=[
+            pltpu.VMEM((10, 2048), f32),
+            pltpu.VMEM((TILES, 128), f32),
+            pltpu.VMEM((10, 16), i32),
+            pltpu.VMEM((10, TRAIL), i32),
             pltpu.VMEM((10, TILES, 128), f32),
             pltpu.VMEM((343, TILES, 128), f32),
             pltpu.VMEM((343, TILES, 128), f32),
@@ -281,9 +333,6 @@
             pltpu.VMEM((RING, 10, 16), i32),
             pltpu.VMEM((4, RING, 16), i32),
             pltpu.SMEM((4, RING, 16), i32),
-            pltpu.VMEM((2048, TRAIL), f32),
-            pltpu.VMEM((2048, PANEL), f32),
-            pltpu.VMEM((2048, TRAIL), f32),
             pltpu.VMEM((RING,) + chunk, f32),
             pltpu.VMEM((RING - 1,) + chunk, f32),
             pltpu.VMEM((RING,) + chunk, f32),
@@ -293,18 +342,29 @@
             pltpu.VMEM((RING,) + wide, f32),
             pltpu.VMEM((RING,) + wide, f32),
             pltpu.VMEM((PANEL, PANEL), f32),
+            dma((4,)),
             dma,
             dma,
             dma,
             dma((6,)),
             dma((6,)),
-            dma,
         ],
         name="panel_step",
         compiler_params=pltpu.CompilerParams(
-            collective_id=0, has_side_effects=True, vmem_limit_bytes=40 * 2**20
+            collective_id=0, has_side_effects=True, vmem_limit_bytes=32 * 2**20
         ),
-    )(points, run_weights.reshape(TILES, 128), panel_degrees, trailing_degrees)
+    )(*(pltpu.with_memory_space_constraint(a, pltpu.HBM) for a in (
+        points, run_weights.reshape(TILES, 128), panel_degrees, trailing_degrees
+    )))
+    return pl.pallas_call(
+        update_kernel,
+        out_shape=[upper, coupling, updated],
+        in_specs=[vmem] * 5,
+        out_specs=[hbm] * 3,
+        scratch_shapes=[pltpu.VMEM((2048, TRAIL), f32), dma((6,))],
+        name="update_step",
+        compiler_params=pltpu.CompilerParams(vmem_limit_bytes=16 * 2**20),
+    )(*parts)
 
 
 def solution(mesh):

time: 54.9 us -> 43.9 us (0.80)
  local copies, waits for them, and re-layouts: 5.61 us -> 0 us
  Pallas kernels: 48.3 us -> 43.2 us
    unnamed x11 -> x0, local copies, waits for them, and re-layouts: 5.61 us -> none
    pallas_call x1 -> x2, Pallas kernels: 48.3 us -> 43.2 us  [the longest x1 41.3 us: shards(): pl.pallas_call(functools.partial(kernel, run_total), out_shape=[upper, co...]
where the time goes in v2:
time: 43.9 us; the launch traced here: 43.8 us
  Pallas kernels  43.2 us (98%)
  between operations  0.64 us (1%)
    pallas_call x1, Pallas kernels, shards(): pl.pallas_call(functools.partial(kernel, run_total), out_shape=[upper, co...  41.3 us
    pallas_call x1, Pallas kernels, shards(): pl.pallas_call(update_kernel, out_shape=[upper, coupling, updated], in_sp...  1.83 us

profile of v2, /device:TPU:1, one launch (start us, length us, event | category | flops | bytes accessed | tf_op | source)
XLA Modules:
  0.0 43.8 jit_solution(16009116336239256920)
XLA Ops:
  0.6 41.3 %panel_step.1 = (f32[128,128]{1,0:T(8,128)S(1)}, f32[128,256]{1,0:T(8,128)S(1)}, f32[128,256]{1,0:T(8,128)S(1)}, f32[2048,256]{1,0:T(8,128)S(1)}, bf16[2048,256]{1,0:T(8,128)(2,1)S(1)}) custom-call(f32[10,2048]{1,0:T(8,128)} %points_ref.1, f32[16,128]{1,0:T(8,128)} %bitcast.1, s32[10,16]{1,0:T(8,128)} %panel_deg_ref.1, s32[10,256]{1,0:T(8,128)} %trail_deg_ref.1), custom_call_target="tpu_custom_call" | custom-call | tf_op jit(solution)/shard_map/panel_step/pallas_call | solution.py:315
  42.0 1.8 %update_step.1 = (f32[128,128]{1,0:T(8,128)}, f32[128,256]{1,0:T(8,128)}, f32[2048,256]{1,0:T(8,128)}) custom-call(f32[128,128]{1,0:T(8,128)S(1)} %get-tuple-element.8.upper_ref, f32[128,256]{1,0:T(8,128)S(1)} %get-tuple-element.9.coupling_ref, f32[128,256]{1,0:T(8,128)S(1)} %get-tuple-element.10.weights_ref, f32[2048,256]{1,0:T(8,128)S(1)} %get-tuple-element.11.trail_t, ...), custom_call_target="tpu_custom_call" | custom-call | tf_op jit(solution)/shard_map/update_step/pallas_call | solution.py:359

commit v3 on v2

--- a/solution.py
+++ b/solution.py
@@ -14,74 +14,77 @@
 PANEL = 128
 TRAIL = 256
 COLS = PANEL + TRAIL
+PITCH = COLS + 8
+FAR_FIRST = (4, 3, 5, 2, 6, 1, 7)
 RING = 8
 MESH = pl.DeviceIdType.MESH
-HIGHEST = lax.Precision.HIGHEST
 NN = (((1,), (0,)), ((), ()))
 NT = (((1,), (1,)), ((), ()))
 TN = (((0,), (0,)), ((), ()))
 
 
-def dot(left, right, dims):
-    return lax.dot_general(left, right, dims, precision=HIGHEST, preferred_element_type=jnp.float32)
-
-
 def lane_splat(row, lane):
     return jnp.broadcast_to(row[:, lane:lane + 1], (8, 128))
 
 
-def sublane_splat(row, sublane):
-    return jnp.broadcast_to(row[sublane:sublane + 1, :], (8, 128))
-
-
-def cholesky(gram_ref, upper_ref, inverse_ref):
+def cholesky(gram_ref, upper_ref, inverse_ref, rows_ref):
     sub = lax.broadcasted_iota(jnp.int32, (8, 128), 0)
     lane = lax.broadcasted_iota(jnp.int32, (8, 128), 1)
-    gram = [gram_ref[8 * i:8 * i + 8, :] for i in range(16)]
-    ident = [jnp.where(lane == sub + 8 * i, 1.0, 0.0) for i in range(16)]
+    rows = [gram_ref[8 * i:8 * i + 8, :] for i in range(16)]
+
+    def all_sublanes(row):
+        return jnp.broadcast_to(rows_ref[row:row + 1, :], (8, 128))
+
     for k in range(16):
-        splats = [lane_splat(gram[k], 8 * k + j) for j in range(8)]
-        diag = [[sublane_splat(splats[j], i) if i >= j else None for j in range(8)] for i in range(8)]
+        first, last = 8 * k, k == 15
+        mid = (lane >= first) & (lane < first + 8)
+        for j in range(8):
+            rows_ref[8 * j:8 * j + 8, :] = lane_splat(rows[k], first + j)
+        rows_ref[64:72, :] = rows[k]
+        diag = [[all_sublanes(8 * j + i) if i >= j else None for j in range(8)] for i in range(8)]
+        up = [all_sublanes(64 + j) for j in range(8)]
+        lo = [jnp.where(mid, jnp.where(lane == first + j, 1.0, 0.0), up[j]) for j in range(8)]
+        following = None if last else [lane_splat(rows[k + 1], first + j) for j in range(8)]
         low = [[None] * 8 for _ in range(8)]
         inv = [None] * 8
+        change = None
         for j in range(8):
             inv[j] = lax.rsqrt(diag[j][j])
+            up[j] = up[j] * inv[j]
+            lo[j] = lo[j] * inv[j]
             for i in range(j + 1, 8):
                 low[i][j] = diag[i][j] * inv[j]
+            if not last:
+                following[j] = following[j] * inv[j]
+                term = following[j] * lo[j]
+                change = term if change is None else change + term
             for i in range(j + 1, 8):
                 for m in range(i, 8):
                     diag[m][i] = diag[m][i] - low[m][j] * low[i][j]
-        up, lo = [], []
-        for j in range(8):
-            a, b = sublane_splat(gram[k], j), sublane_splat(ident[k], j)
-            for i in range(j):
-                a = a - low[j][i] * up[i]
-                b = b - low[j][i] * lo[i]
-            up.append(a * inv[j])
-            lo.append(b * inv[j])
+                up[i] = up[i] - low[i][j] * up[j]
+                lo[i] = lo[i] - low[i][j] * lo[j]
+                if not last:
+                    following[i] = following[i] - low[i][j] * following[j]
         up_rows, lo_rows = up[0], lo[0]
         for j in range(1, 8):
             up_rows = jnp.where(sub == j, up[j], up_rows)
             lo_rows = jnp.where(sub == j, lo[j], lo_rows)
-        upper_ref[8 * k:8 * k + 8, :] = jnp.where(lane >= sub + 8 * k, up_rows, 0.0)
-        inverse_ref[8 * k:8 * k + 8, :] = lo_rows
-        if k == 15:
+        upper_ref[first:first + 8, :] = jnp.where(lane >= sub + first, up_rows, 0.0)
+        inverse_ref[first:first + 8, :] = jnp.where(lane < first + 8, lo_rows, 0.0)
+        if last:
             break
+        rows[k + 1] = jnp.where(mid, 0.0, rows[k + 1]) - change
+        if k == 14:
+            continue
         for j in reversed(range(8)):
-            for i in range(j + 1, 8):
-                up[j] = up[j] - low[i][j] * up[i]
-                lo[j] = lo[j] - low[i][j] * lo[i]
-            up[j] = up[j] * inv[j]
             lo[j] = lo[j] * inv[j]
-        for i in range(k + 1, 16):
+            for i in range(j):
+                lo[i] = lo[i] - low[j][i] * lo[j]
+        for i in range(k + 2, 16):
+            kept = jnp.where(mid, 0.0, rows[i])
             for j in range(8):
-                c = lane_splat(gram[i], 8 * k + j)
-                if j == 0:
-                    a, b = c * up[0], c * lo[0]
-                else:
-                    a, b = a + c * up[j], b + c * lo[j]
-            gram[i] = gram[i] - a
-            ident[i] = ident[i] - b
+                kept = kept - lane_splat(rows[i], first + j) * lo[j]
+            rows[i] = kept
 
 
 def legendre(coord):
@@ -128,11 +131,11 @@
 
 def kernel(run_total, points_ref, weights_ref, panel_deg_ref, trail_deg_ref,
            upper_out, coupling_out, weights_out, trail_t, panel_t,
-           points_v, weights_v, panel_deg_v, trail_deg_v,
+           points_v, weights_v, trail_deg_v,
            coords, triple_a, triple_b, pair_a, pair_b, columns,
-           trail_idx_v, trail_idx, panel_degs, panel_idx_v, panel_idx,
+           trail_idx_v, trail_idx, panel_degs,
            gram_x, gram_land, gram_z, gram_all, cross_x, cross_land, cross_z, cross_all,
-           inverse, in_sem, local_sem, deg_send, deg_recv, send_sem, recv_sem):
+           inverse, rows_v, in_sem, local_sem, deg_send, deg_recv, send_sem, recv_sem):
     s, y = lax.axis_index("sample"), lax.axis_index("basis")
     z, q = s // RING, lax.rem(s, RING)
     others = range(1, RING)
@@ -141,12 +144,13 @@
     z_peers = [(lax.rem(z + k, RING) * RING + q, y) for k in others]
 
     barrier = pltpu.get_barrier_semaphore()
-    for peer in y_peers + z_peers + q_peers:
-        pl.semaphore_signal(barrier, inc=1, device_id=peer, device_id_type=MESH)
+    for k in FAR_FIRST:
+        for peers in (y_peers, z_peers, q_peers):
+            pl.semaphore_signal(barrier, inc=1, device_id=peers[k - 1], device_id_type=MESH)
     loads = [
         pltpu.make_async_copy(src, dst, in_sem.at[i])
         for i, (src, dst) in enumerate([
-            (panel_deg_ref, panel_deg_v), (trail_deg_ref, trail_deg_v), (points_ref, points_v), (weights_ref, weights_v)
+            (panel_deg_ref, panel_degs.at[y]), (trail_deg_ref, trail_deg_v), (points_ref, points_v), (weights_ref, weights_v)
         ])
     ]
     for load in loads:
@@ -162,9 +166,8 @@
 
     loads[0].wait()
     pl.semaphore_wait(barrier, 3 * (RING - 1))
-    for peer in y_peers:
-        send(panel_deg_v, panel_degs.at[y], deg_send, deg_recv, peer)
-    panel_degs[y] = panel_deg_v[...]
+    for k in FAR_FIRST:
+        send(panel_degs.at[y], panel_degs.at[y], deg_send.at[k - 1], deg_recv.at[k - 1], y_peers[k - 1])
 
     loads[1].wait()
     for g, row in enumerate(table_rows(lambda d: trail_deg_v[d:d + 1, :])):
@@ -184,38 +187,28 @@
 
     def trail_column(j, carry):
         value = product(trail_idx[0, j], trail_idx[1, j], trail_idx[2, j], trail_idx[3, j])
-        columns[pl.ds(PANEL + j, TILES, stride=COLS), :] = value
+        columns[pl.ds(PANEL + j, TILES, stride=PITCH), :] = value
         return carry
 
     lax.fori_loop(0, TRAIL, trail_column, 0, unroll=8)
-    scale = math.sqrt(run_total)
-
-    def transpose_trail(r, carry):
-        rows = pl.ds(pl.multiple_of(r * 128, 128), 128)
-        base = pl.multiple_of(r * COLS, 128)
-        trail_t[rows, :] = columns[pl.ds(base + PANEL, TRAIL), :].T * scale
-        return carry
-
-    lax.fori_loop(0, TILES, transpose_trail, 0)
-
-    wait(panel_degs.at[pl.ds(0, RING - 1)], deg_recv)
-    for g, rows in enumerate(table_rows(lambda d: panel_degs[:, d, :])):
-        panel_idx_v[g] = rows
-    panel_copy = pltpu.make_async_copy(panel_idx_v, panel_idx, local_sem)
-    panel_copy.start()
-    panel_copy.wait()
-
-    def panel_column(o, carry):
-        for i in range(16):
-            value = product(panel_idx[0, o, i], panel_idx[1, o, i], panel_idx[2, o, i], panel_idx[3, o, i])
-            columns[pl.ds(o * 16 + i, TILES, stride=COLS), :] = value
-        return carry
-
-    lax.fori_loop(0, RING, panel_column, 0)
+
+    def panel_block(owner):
+        def panel_column(i, carry):
+            rows = table_rows(lambda d: panel_degs[owner, d, i])
+            columns[pl.ds(owner * 16 + i, TILES, stride=PITCH), :] = product(*rows)
+            return carry
+
+        lax.fori_loop(0, 16, panel_column, 0, unroll=4)
+
+    panel_block(y)
+    for k in (1, 7, 2, 6, 3, 5, 4):
+        owner = lax.rem(y + RING - k, RING)
+        wait(panel_degs.at[owner], deg_recv.at[k - 1])
+        panel_block(owner)
 
     def block(start, size, r):
         high, low = split(jnp.concatenate(
-            [columns[pl.ds((2 * r + h) * COLS + start, size), :] for h in range(2)], axis=1
+            [columns[pl.ds((2 * r + h) * PITCH + start, size), :] for h in range(2)], axis=1
         ))
         return jnp.concatenate([high, low], axis=0)
 
@@ -224,7 +217,7 @@
         return (total[rows:, cols:] + (total[:rows, cols:] + total[rows:, :cols])) + total[:rows, :cols]
 
     def phase_one(x, land, i):
-        for k in others:
+        for k in FAR_FIRST:
             send(x.at[lax.rem(q + k, RING)], land.at[k - 1], send_sem.at[i], recv_sem.at[i], q_peers[k - 1])
 
     def phase_two(x, land, all_z, i):
@@ -233,8 +226,8 @@
         for k in range(RING - 1):
             part = part + land[k]
         all_z[z] = part
-        for peer in z_peers:
-            send(all_z.at[z], all_z.at[z], send_sem.at[i + 1], recv_sem.at[i + 1], peer)
+        for k in FAR_FIRST:
+            send(all_z.at[z], all_z.at[z], send_sem.at[i + 1], recv_sem.at[i + 1], z_peers[k - 1])
 
     def phase_three(land, all_z, out, i):
         wait(land, recv_sem.at[i + 1])
@@ -242,8 +235,8 @@
         for k in others:
             total = total + all_z[k]
         out[q] = total
-        for peer in q_peers:
-            send(out.at[q], out.at[q], send_sem.at[i + 2], recv_sem.at[i + 2], peer)
+        for k in FAR_FIRST:
+            send(out.at[q], out.at[q], send_sem.at[i + 2], recv_sem.at[i + 2], q_peers[k - 1])
 
     panels = [block(0, PANEL, r) for r in range(TILES // 2)]
     gram = fast_dot(panels[0], panels[0], NT)
@@ -257,26 +250,34 @@
     cross_x[...] = quadrants(cross).reshape(cross_x.shape)
     phase_one(cross_x, cross_land, 3)
 
-    def transpose_panel(r, carry):
+    scale = math.sqrt(run_total)
+
+    def transpose(r, carry):
         rows = pl.ds(pl.multiple_of(r * 128, 128), 128)
-        base = pl.multiple_of(r * COLS, 128)
+        base = pl.multiple_of(r * PITCH, 8)
         high, low = split(columns[pl.ds(base, PANEL), :].T)
         panel_t[rows, :] = jnp.concatenate([high, low], axis=1)
+        trail_t[rows, :] = columns[pl.ds(base + PANEL, TRAIL), :].T * scale
         return carry
 
-    lax.fori_loop(0, TILES, transpose_panel, 0)
     phase_two(gram_x, gram_land, gram_z, 0)
     phase_two(cross_x, cross_land, cross_z, 3)
+    lax.fori_loop(0, TILES, transpose, 0)
     phase_three(gram_land, gram_z, gram_all, 0)
     phase_three(cross_land, cross_z, cross_all, 3)
 
     wait(gram_land, recv_sem.at[2])
-    cholesky(gram_all.reshape(PANEL, PANEL), upper_out, inverse)
+    cholesky(gram_all.reshape(PANEL, PANEL), upper_out, inverse, rows_v)
     wait(cross_land, recv_sem.at[5])
-    coupling = dot(inverse[...], cross_all[...].reshape(PANEL, TRAIL), NN)
+    inv_high, inv_low = split(inverse[...])
+    high, low = split(cross_all[...].reshape(PANEL, TRAIL))
+    coupling = fast_dot(inv_high, high, NN) + (fast_dot(inv_high, low, NN) + fast_dot(inv_low, high, NN))
     coupling_out[...] = coupling
-    weights_out[...] = dot(inverse[...], coupling, TN) * -scale
-    wait(panel_degs.at[pl.ds(0, RING - 1)], deg_send)
+    high, low = split(coupling)
+    weights = fast_dot(inv_high, high, TN) + (fast_dot(inv_high, low, TN) + fast_dot(inv_low, high, TN))
+    weights_out[...] = weights * -scale
+    for k in others:
+        wait(panel_degs.at[y], deg_send.at[k - 1])
     for i in range(3):
         wait(gram_land, send_sem.at[i])
         wait(cross_land, send_sem.at[i + 3])
@@ -291,9 +292,9 @@
         copy.start()
     high, low = split(weights_ref[...])
     both = jnp.concatenate([high, high], axis=0)
-    part = 2048 // 4
+    part = 2048 // 8
     large = []
-    for p in range(4):
+    for p in range(8):
         rows = pl.ds(p * part, part)
         panel = panel_t[rows, :]
         buf[rows, :] = trail_t[rows, :] + (fast_dot(panel[:, :PANEL], low, NN) + fast_dot(panel, both, NN))
@@ -320,19 +321,16 @@
         scratch_shapes=[
             pltpu.VMEM((10, 2048), f32),
             pltpu.VMEM((TILES, 128), f32),
-            pltpu.VMEM((10, 16), i32),
             pltpu.VMEM((10, TRAIL), i32),
             pltpu.VMEM((10, TILES, 128), f32),
             pltpu.VMEM((343, TILES, 128), f32),
             pltpu.VMEM((343, TILES, 128), f32),
             pltpu.VMEM((49, TILES, 128), f32),
             pltpu.VMEM((49, TILES, 128), f32),
-            pltpu.VMEM((TILES * COLS, 128), f32),
+            pltpu.VMEM((TILES * PITCH, 128), f32),
             pltpu.VMEM((4, TRAIL), i32),
             pltpu.SMEM((4, TRAIL), i32),
-            pltpu.VMEM((RING, 10, 16), i32),
-            pltpu.VMEM((4, RING, 16), i32),
-            pltpu.SMEM((4, RING, 16), i32),
+            pltpu.SMEM((RING, 10, 16), i32),
             pltpu.VMEM((RING,) + chunk, f32),
             pltpu.VMEM((RING - 1,) + chunk, f32),
             pltpu.VMEM((RING,) + chunk, f32),
@@ -342,10 +340,11 @@
             pltpu.VMEM((RING,) + wide, f32),
             pltpu.VMEM((RING,) + wide, f32),
             pltpu.VMEM((PANEL, PANEL), f32),
+            pltpu.VMEM((72, 128), f32),
             dma((4,)),
             dma,
-            dma,
-            dma,
+            dma((RING - 1,)),
+            dma((RING - 1,)),
             dma((6,)),
             dma((6,)),
         ],
@@ -361,7 +360,7 @@
         out_shape=[upper, coupling, updated],
         in_specs=[vmem] * 5,
         out_specs=[hbm] * 3,
-        scratch_shapes=[pltpu.VMEM((2048, TRAIL), f32), dma((6,))],
+        scratch_shapes=[pltpu.VMEM((2048, TRAIL), f32), dma((10,))],
         name="update_step",
         compiler_params=pltpu.CompilerParams(vmem_limit_bytes=16 * 2**20),
     )(*parts)

time: 43.9 us -> 40.6 us (0.925)
  Pallas kernels: 43.2 us -> 39.8 us
    pallas_call x1, Pallas kernels: 41.3 us -> 38.1 us  [shards(): pl.pallas_call(functools.partial(kernel, run_total), out_shape=[upper, co...]
where the time goes in v3:
time: 40.6 us; the launch traced here: 40.4 us
  Pallas kernels  39.8 us (98%)
  between operations  0.64 us (2%)
    pallas_call x1, Pallas kernels, shards(): pl.pallas_call(functools.partial(kernel, run_total), out_shape=[upper, co...  38.1 us
    pallas_call x1, Pallas kernels, shards(): pl.pallas_call(update_kernel, out_shape=[upper, coupling, updated], in_sp...  1.7 us

profile of v3, /device:TPU:1, one launch (start us, length us, event | category | flops | bytes accessed | tf_op | source)
XLA Modules:
  0.0 40.4 jit_solution(2659181572844944086)
XLA Ops:
  0.6 38.1 %panel_step.1 = (f32[128,128]{1,0:T(8,128)S(1)}, f32[128,256]{1,0:T(8,128)S(1)}, f32[128,256]{1,0:T(8,128)S(1)}, f32[2048,256]{1,0:T(8,128)S(1)}, bf16[2048,256]{1,0:T(8,128)(2,1)S(1)}) custom-call(f32[10,2048]{1,0:T(8,128)} %points_ref.1, f32[16,128]{1,0:T(8,128)} %bitcast.1, s32[10,16]{1,0:T(8,128)} %panel_deg_ref.1, s32[10,256]{1,0:T(8,128)} %trail_deg_ref.1), custom_call_target="tpu_custom_call" | custom-call | tf_op jit(solution)/shard_map/panel_step/pallas_call | solution.py:316
  38.7 1.7 %update_step.1 = (f32[128,128]{1,0:T(8,128)}, f32[128,256]{1,0:T(8,128)}, f32[2048,256]{1,0:T(8,128)}) custom-call(f32[128,128]{1,0:T(8,128)S(1)} %get-tuple-element.8.upper_ref, f32[128,256]{1,0:T(8,128)S(1)} %get-tuple-element.9.coupling_ref, f32[128,256]{1,0:T(8,128)S(1)} %get-tuple-element.10.weights_ref, f32[2048,256]{1,0:T(8,128)S(1)} %get-tuple-element.11.trail_t, ...), custom_call_target="tpu_custom_call" | custom-call | tf_op jit(solution)/shard_map/update_step/pallas_call | solution.py:358

commit v4 on v3

--- a/solution.py
+++ b/solution.py
@@ -164,10 +164,17 @@
     def wait(ref, sem):
         pltpu.make_async_copy(ref, ref, sem).wait()
 
-    loads[0].wait()
-    pl.semaphore_wait(barrier, 3 * (RING - 1))
-    for k in FAR_FIRST:
-        send(panel_degs.at[y], panel_degs.at[y], deg_send.at[k - 1], deg_recv.at[k - 1], y_peers[k - 1])
+    away = jnp.minimum(y, RING - y)
+
+    def exchange_degrees(now):
+        @pl.when(now)
+        def _():
+            loads[0].wait()
+            pl.semaphore_wait(barrier, 3 * (RING - 1))
+            for k in FAR_FIRST:
+                send(panel_degs.at[y], panel_degs.at[y], deg_send.at[k - 1], deg_recv.at[k - 1], y_peers[k - 1])
+
+    exchange_degrees(away >= 3)
 
     loads[1].wait()
     for g, row in enumerate(table_rows(lambda d: trail_deg_v[d:d + 1, :])):
@@ -180,6 +187,7 @@
         coords[:, r, :] = points_v[:, 128 * r:128 * r + 128]
     weight = jnp.sqrt(weights_v[...] / run_total)
     fill_tables(coords, weight, (triple_a, triple_b), (pair_a, pair_b))
+    exchange_degrees(jnp.logical_and(away > 0, away < 3))
     idx_copy.wait()
 
     def product(i, j, k, m):
@@ -191,6 +199,7 @@
         return carry
 
     lax.fori_loop(0, TRAIL, trail_column, 0, unroll=8)
+    exchange_degrees(away == 0)
 
     def panel_block(owner):
         def panel_column(i, carry):
@@ -291,13 +300,14 @@
     for copy in small:
         copy.start()
     high, low = split(weights_ref[...])
-    both = jnp.concatenate([high, high], axis=0)
-    part = 2048 // 8
+    stacked = jnp.concatenate([high, high, low], axis=0)
+    part = 2048 // 16
     large = []
-    for p in range(8):
+    for p in range(16):
         rows = pl.ds(p * part, part)
         panel = panel_t[rows, :]
-        buf[rows, :] = trail_t[rows, :] + (fast_dot(panel[:, :PANEL], low, NN) + fast_dot(panel, both, NN))
+        panel = jnp.concatenate([panel, panel[:, :PANEL]], axis=1)
+        buf[rows, :] = trail_t[rows, :] + fast_dot(panel, stacked, NN)
         large.append(pltpu.make_async_copy(buf.at[rows, :], updated_out.at[rows, :], sem.at[2 + p]))
         large[-1].start()
     for copy in small + large:
@@ -360,7 +370,7 @@
         out_shape=[upper, coupling, updated],
         in_specs=[vmem] * 5,
         out_specs=[hbm] * 3,
-        scratch_shapes=[pltpu.VMEM((2048, TRAIL), f32), dma((10,))],
+        scratch_shapes=[pltpu.VMEM((2048, TRAIL), f32), dma((18,))],
         name="update_step",
         compiler_params=pltpu.CompilerParams(vmem_limit_bytes=16 * 2**20),
     )(*parts)

time: 40.6 us -> 39.8 us (0.980)
  Pallas kernels: 39.8 us -> 39 us
    pallas_call x1, Pallas kernels: 38.1 us -> 37.3 us  [shards(): pl.pallas_call(functools.partial(kernel, run_total), out_shape=[upper, co...]
where the time goes in v4:
time: 39.8 us; the launch traced here: 39.7 us
  Pallas kernels  39 us (98%)
  between operations  0.64 us (2%)
    pallas_call x1, Pallas kernels, shards(): pl.pallas_call(functools.partial(kernel, run_total), out_shape=[upper, co...  37.3 us
    pallas_call x1, Pallas kernels, shards(): pl.pallas_call(update_kernel, out_shape=[upper, coupling, updated], in_sp...  1.7 us

profile of v4, /device:TPU:1, one launch (start us, length us, event | category | flops | bytes accessed | tf_op | source)
XLA Modules:
  0.0 39.7 jit_solution(14200679743946790631)
XLA Ops:
  0.6 37.3 %panel_step.1 = (f32[128,128]{1,0:T(8,128)S(1)}, f32[128,256]{1,0:T(8,128)S(1)}, f32[128,256]{1,0:T(8,128)S(1)}, f32[2048,256]{1,0:T(8,128)S(1)}, bf16[2048,256]{1,0:T(8,128)(2,1)S(1)}) custom-call(f32[10,2048]{1,0:T(8,128)} %points_ref.1, f32[16,128]{1,0:T(8,128)} %bitcast.1, s32[10,16]{1,0:T(8,128)} %panel_deg_ref.1, s32[10,256]{1,0:T(8,128)} %trail_deg_ref.1), custom_call_target="tpu_custom_call" | custom-call | tf_op jit(solution)/shard_map/panel_step/pallas_call | solution.py:326
  38.0 1.7 %update_step.1 = (f32[128,128]{1,0:T(8,128)}, f32[128,256]{1,0:T(8,128)}, f32[2048,256]{1,0:T(8,128)}) custom-call(f32[128,128]{1,0:T(8,128)S(1)} %get-tuple-element.8.upper_ref, f32[128,256]{1,0:T(8,128)S(1)} %get-tuple-element.9.coupling_ref, f32[128,256]{1,0:T(8,128)S(1)} %get-tuple-element.10.weights_ref, f32[2048,256]{1,0:T(8,128)S(1)} %get-tuple-element.11.trail_t, ...), custom_call_target="tpu_custom_call" | custom-call | tf_op jit(solution)/shard_map/update_step/pallas_call | solution.py:368

commit v5 on v4

--- a/solution.py
+++ b/solution.py
@@ -135,7 +135,7 @@
            coords, triple_a, triple_b, pair_a, pair_b, columns,
            trail_idx_v, trail_idx, panel_degs,
            gram_x, gram_land, gram_z, gram_all, cross_x, cross_land, cross_z, cross_all,
-           inverse, rows_v, in_sem, local_sem, deg_send, deg_recv, send_sem, recv_sem):
+           inverse, rows_v, trail_halves, in_sem, local_sem, deg_send, deg_recv, send_sem, recv_sem):
     s, y = lax.axis_index("sample"), lax.axis_index("basis")
     z, q = s // RING, lax.rem(s, RING)
     others = range(1, RING)
@@ -209,17 +209,20 @@
 
         lax.fori_loop(0, 16, panel_column, 0, unroll=4)
 
+    def block(start, size, r):
+        high, low = split(jnp.concatenate(
+            [columns[pl.ds((2 * r + h) * PITCH + start, size), :] for h in range(2)], axis=1
+        ))
+        return jnp.concatenate([high, low], axis=0)
+
+    for r in range(TILES // 2):
+        trail_halves[r] = block(PANEL, TRAIL, r)
+
     panel_block(y)
     for k in (1, 7, 2, 6, 3, 5, 4):
         owner = lax.rem(y + RING - k, RING)
         wait(panel_degs.at[owner], deg_recv.at[k - 1])
         panel_block(owner)
-
-    def block(start, size, r):
-        high, low = split(jnp.concatenate(
-            [columns[pl.ds((2 * r + h) * PITCH + start, size), :] for h in range(2)], axis=1
-        ))
-        return jnp.concatenate([high, low], axis=0)
 
     def quadrants(total):
         rows, cols = total.shape[0] // 2, total.shape[1] // 2
@@ -255,7 +258,7 @@
     phase_one(gram_x, gram_land, 0)
     cross = jnp.zeros((2 * PANEL, 2 * TRAIL), jnp.float32)
     for r in range(TILES // 2):
-        cross = cross + fast_dot(panels[r], block(PANEL, TRAIL, r), NT)
+        cross = cross + fast_dot(panels[r], trail_halves[r], NT)
     cross_x[...] = quadrants(cross).reshape(cross_x.shape)
     phase_one(cross_x, cross_land, 3)
 
@@ -351,6 +354,7 @@
             pltpu.VMEM((RING,) + wide, f32),
             pltpu.VMEM((PANEL, PANEL), f32),
             pltpu.VMEM((72, 128), f32),
+            pltpu.VMEM((TILES // 2, 2 * TRAIL, 256), jnp.bfloat16),
             dma((4,)),
             dma,
             dma((RING - 1,)),

time: 39.8 us -> 39.8 us (level)
  no operation moved by 1% of the time
where the time goes in v5:
time: 39.8 us; the launch traced here: 39.7 us
  Pallas kernels  39 us (98%)
  between operations  0.64 us (2%)
    pallas_call x1, Pallas kernels, shards(): pl.pallas_call(functools.partial(kernel, run_total), out_shape=[upper, co...  37.3 us
    pallas_call x1, Pallas kernels, shards(): pl.pallas_call(update_kernel, out_shape=[upper, coupling, updated], in_sp...  1.69 us

profile of v5, /device:TPU:1, one launch (start us, length us, event | category | flops | bytes accessed | tf_op | source)
XLA Modules:
  0.0 39.7 jit_solution(1656103454009640394)
XLA Ops:
  0.6 37.3 %panel_step.1 = (f32[128,128]{1,0:T(8,128)S(1)}, f32[128,256]{1,0:T(8,128)S(1)}, f32[128,256]{1,0:T(8,128)S(1)}, f32[2048,256]{1,0:T(8,128)S(1)}, bf16[2048,256]{1,0:T(8,128)(2,1)S(1)}) custom-call(f32[10,2048]{1,0:T(8,128)} %points_ref.1, f32[16,128]{1,0:T(8,128)} %bitcast.1, s32[10,16]{1,0:T(8,128)} %panel_deg_ref.1, s32[10,256]{1,0:T(8,128)} %trail_deg_ref.1), custom_call_target="tpu_custom_call" | custom-call | tf_op jit(solution)/shard_map/panel_step/pallas_call | solution.py:329
  38.0 1.7 %update_step.1 = (f32[128,128]{1,0:T(8,128)}, f32[128,256]{1,0:T(8,128)}, f32[2048,256]{1,0:T(8,128)}) custom-call(f32[128,128]{1,0:T(8,128)S(1)} %get-tuple-element.8.upper_ref, f32[128,256]{1,0:T(8,128)S(1)} %get-tuple-element.9.coupling_ref, f32[128,256]{1,0:T(8,128)S(1)} %get-tuple-element.10.weights_ref, f32[2048,256]{1,0:T(8,128)S(1)} %get-tuple-element.11.trail_t, ...), custom_call_target="tpu_custom_call" | custom-call | tf_op jit(solution)/shard_map/update_step/pallas_call | solution.py:372
